TPU v7x, 512 devices: a whole 4x4x16 slice. The times are simulated.
512 devices in a mesh: depth: 16 (over x_hi, y, core), tile: 32 (over z, x_lo).
Axes of the slice: x: 4 (x_hi: 2, x_lo: 2; x = x_hi * 2 + x_lo), y: 4, z: 16, core: 2. Of those that a mesh axis runs over, the one named last changes fastest.
Arguments:
- volume: float32 [16, 1024, 1024], P('depth', 'tile'), may hold values from 0.05 to 100
- measured: float32 [1024, 1024], P('tile'), may hold values from 0.15 to 0.6
- point_spread: bfloat16 [16, 13, 13], P('depth'), may hold values from 7.390976e-05 to 0.0007362366
- entry_block: int32 [32, 4096], P('tile', 'depth'), may hold values from 0 to 63
- entry_neuron: int32 [32, 4096], P('tile', 'depth'), may hold values from -1 to 8191, as said below
- footprints: bfloat16 [32, 4096, 4, 128], P('tile', 'depth'), may hold values from 0.049804688 to 1
- seed_plane: int32 [8192], replicated, may hold values from 0 to 15
- seed_row: int32 [8192], replicated, may hold values from 0 to 1023
- seed_col: int32 [8192], replicated, may hold values from 0 to 1023
- owner_slot: int32 [8192], replicated, may hold values from 0 to 8191, each once
Outputs:
- estimate: float32 [16, 1024, 1024], P('depth', 'tile')
- demixed: float32 [8192], P(('depth', 'tile'))
Inputs may be any that keep to these rules, and one draw needn't show every extreme that they name: `entry_neuron`: -1 marks an empty slot; on each device the active slots come first, from 85 to 256 of them, and some device has all 256 slots active; neuron ids may repeat.
All inputs are finite; a program needn't handle non-finite values.
Results may differ from a plain program's by a relative error of at most 0.0025.
Values may be sent and summed in bfloat16 or wider, within the bound.
No kernel may reach another device: no remote copies, remote signals or barrier semaphores. Data moves between devices by JAX's collectives and lax.ppermute only.
A program may use at most 64 MiB of HBM per device.

v0:
```python
import jax
import jax.numpy as jnp
from jax import lax
from jax.sharding import PartitionSpec as P

ITERS = 2
RADIUS = 6
BR = 4
CB = 128


def padded_2(cells, sides, width):
    for axis, dim in sides:
        count = lax.axis_size(axis)
        ends = count - 1
        head = lax.slice_in_dim(cells, 0, width, axis=dim)
        tail = lax.slice_in_dim(cells, cells.shape[dim] - width, cells.shape[dim], axis=dim)
        cells = jnp.concatenate(
            [
                lax.ppermute(tail, axis, [(i, (i + 1) % count) for i in range(ends)]),
                cells,
                lax.ppermute(head, axis, [((i + 1) % count, i) for i in range(ends)]),
            ],
            axis=dim,
        )
    return cells


def band_tables(point_spread):
    kernel_size = point_spread.shape[1]
    radius = kernel_size // 2
    inner = jnp.arange(3 * CB)[:, None, None]
    outer = jnp.arange(CB)[None, :, None]
    tapnum = jnp.arange(kernel_size)[None, None, :]
    ahead_hot = (inner - CB - outer + radius == tapnum).astype(jnp.float32)
    behind_hot = (CB + outer + radius - inner == tapnum).astype(jnp.float32)
    spread_f = point_spread.astype(jnp.float32)
    high = lax.Precision.HIGHEST
    ahead = jnp.einsum("pak,jik->paji", spread_f, ahead_hot, precision=high).astype(jnp.bfloat16)
    behind = jnp.einsum("pak,jik->paji", spread_f, behind_hot, precision=high).astype(jnp.bfloat16)
    return (ahead, behind)


def column_blocks(field):
    shape = field.shape
    blocks = field.reshape(shape[:-1] + (shape[-1] // CB, CB))
    widths = [(0, 0)] * (len(shape) - 1)
    before = jnp.pad(blocks, widths + [(1, 0), (0, 0)])[..., :-1, :]
    after = jnp.pad(blocks, widths + [(0, 1), (0, 0)])[..., 1:, :]
    return jnp.concatenate([before, blocks, after], axis=-1)


def project_ahead(padded, ahead, rows_dev):
    stacked = column_blocks(padded)
    kernel_size = ahead.shape[1]
    summed = None
    for tapnum in range(kernel_size):
        term = jnp.einsum(
            "prnj,pji->rni",
            stacked[:, tapnum : tapnum + rows_dev],
            ahead[:, tapnum],
            preferred_element_type=jnp.float32,
        )
        summed = term if summed is None else summed + term
    return summed.reshape(rows_dev, -1)


def project_behind(padded, behind, rows_dev):
    stacked = column_blocks(padded)
    kernel_size = behind.shape[1]
    last = kernel_size - 1
    summed = None
    for tapnum in range(kernel_size):
        begin = last - tapnum
        term = jnp.einsum(
            "rnj,pji->prni",
            stacked[begin : begin + rows_dev],
            behind[:, tapnum],
            preferred_element_type=jnp.float32,
        )
        summed = term if summed is None else summed + term
    return summed.reshape(behind.shape[0], rows_dev, -1)


def body(
    volume,
    measured,
    point_spread,
    entry_block,
    entry_neuron,
    footprints,
    seed_plane,
    seed_row,
    seed_col,
    owner_slot,
):
    planes_dev, rows_dev, columns = volume.shape
    norm = jnp.sum(point_spread.astype(jnp.float32), axis=(1, 2))
    ahead, behind = band_tables(point_spread)
    estimate = volume
    for sweep in range(ITERS):
        rounded = estimate.astype(jnp.bfloat16)
        padded = padded_2(rounded, (("tile", 1),), RADIUS)
        partial_value = project_ahead(padded, ahead, rows_dev)
        plane_sum = lax.psum(partial_value.astype(jnp.bfloat16), "depth").astype(jnp.float32)
        ratio = (measured / plane_sum).astype(jnp.bfloat16)
        ratio_padded = padded_2(ratio, (("tile", 0),), RADIUS)
        backward = project_behind(ratio_padded, behind, rows_dev)
        estimate = estimate * backward / norm[:, None, None]
    row_groups = rows_dev // BR
    col_groups = columns // CB
    blocked = estimate.reshape(planes_dev, row_groups, BR, col_groups, CB).transpose(0, 1, 3, 2, 4)
    blocked = blocked.reshape(planes_dev * row_groups * col_groups, BR, CB)
    block_ids = entry_block[0]
    neuron = entry_neuron[0]
    weights = footprints[0].astype(jnp.float32)
    active = (neuron >= 0).astype(jnp.float32)
    neurons = seed_plane.shape[0]
    slot_pos = owner_slot[jnp.maximum(neuron, 0)]
    picked = blocked[block_ids]
    slot_proj = jnp.sum(weights * picked, axis=(1, 2)) * active
    proj_dense = jnp.zeros((neurons,), jnp.float32).at[slot_pos].add(slot_proj)
    holder = (seed_plane // planes_dev == lax.axis_index("depth")) & (
        seed_row // rows_dev == lax.axis_index("tile")
    )
    seed_value = estimate[seed_plane % planes_dev, seed_row % rows_dev, seed_col] * holder.astype(
        jnp.float32
    )
    seed_dense = jnp.zeros((neurons,), jnp.float32).at[owner_slot].add(seed_value)
    group = lax.axis_size(("depth", "tile"))
    owned_count = neurons // group
    proj_all, seed_all = lax.psum((proj_dense, seed_dense), ("depth", "tile"))
    offset = lax.axis_index(("depth", "tile")) * owned_count
    proj_own = lax.dynamic_slice_in_dim(proj_all, offset, owned_count, 0)
    seed_own = lax.dynamic_slice_in_dim(seed_all, offset, owned_count, 0)
    scaled = weights * (seed_all[slot_pos] * active)[:, None, None]
    block_count = blocked.shape[0]
    selector = (jnp.arange(block_count)[:, None] == block_ids[None, :]).astype(jnp.float32)
    rebuilt = jnp.dot(
        selector,
        scaled.reshape(scaled.shape[0], BR * CB),
        precision=lax.Precision.HIGHEST,
        preferred_element_type=jnp.float32,
    )
    rebuilt = rebuilt.reshape(block_count, BR, CB)
    slot_over = jnp.sum(weights * rebuilt[block_ids], axis=(1, 2)) * active
    over_dense = jnp.zeros((neurons,), jnp.float32).at[slot_pos].add(slot_over)
    over_own = lax.psum_scatter(over_dense, ("depth", "tile"), scatter_dimension=0, tiled=True)
    demixed = seed_own * proj_own / (over_own + 100.0 * seed_own)
    return (estimate, demixed)


def solution(mesh):
    in_specs = (
        P("depth", "tile", None),
        P("tile", None),
        P("depth", None, None),
        P("tile", "depth"),
        P("tile", "depth"),
        P("tile", "depth", None, None),
        P(),
        P(),
        P(),
        P(),
    )
    out_specs = (P("depth", "tile", None), P(("depth", "tile")))
    return jax.shard_map(body, mesh=mesh, in_specs=in_specs, out_specs=out_specs, check_vma=False)
```

profile of v0, /device:TPU:1, one launch (start us, length us, event | category | flops | bytes accessed | tf_op | source)
XLA Modules:
  0.0 1035.4 jit_solution(12849229935386808176)
XLA Ops:
  7.2 0.9 convert_element_type.84
  8.7 4.5 collective-permute-start
  13.3 1.3 collective-permute-start.1
  14.7 1.6 fusion.7
  16.3 2.7 fusion.173
  19.1 0.9 fusion.6
  20.0 3.2 fusion.172
  23.3 1.7 gather_fusion.1
  29.7 148.9 %all-reduce.14.cloned.1.call-done = bf16[32,1024]{1,0:T(8,128)(2,1)} async-done(((bf16[32,1024]{1,0:T(8,128)(2,1)}), bf16[32,1024]{1,0:T(8,128)(2,1)}) %all-reduce.14.cloned.1.call-update) | async-done | bytes 65552 | tf_op jit(solution)/shard_map/psum | solution.py:105
  179.5 2.3 collective-permute-start.2
  181.9 1.3 collective-permute-start.3
  183.8 3.3 collective-permute-done.3
  187.3 1.2 fusion.41
  188.5 1.2 convolution_add_fusion.35
  193.3 4.4 collective-permute-start.4
  197.7 1.3 collective-permute-start.5
  199.0 3.2 collective-permute-done.5
  206.1 144.1 %all-reduce.16.cloned.1.call-done = bf16[32,1024]{1,0:T(8,128)(2,1)} async-done(((bf16[32,1024]{1,0:T(8,128)(2,1)}), bf16[32,1024]{1,0:T(8,128)(2,1)}) %all-reduce.16.cloned.1.call-update) | async-done | bytes 65552 | tf_op jit(solution)/shard_map/psum | solution.py:105
  351.0 2.2 collective-permute-start.6
  353.2 1.5 collective-permute-start.7
  355.0 3.5 collective-permute-done.7
  362.6 65.0 %gather_fusion = f32[8192]{0:T(1024)S(1)} fusion(f32[1,32,1024]{2,1,0:T(8,128)S(1)} %fusion.44, s32[8192]{0:T(1024)S(1)} %fusion.156), kind=kCustom, calls=%fused_computation | custom fusion | bytes 163840 | tf_op jit(solution)/shard_map/gather | solution.py:126
  427.6 43.2 %scatter_custom_fusion = f32[8192]{0:T(1024)S(1)} fusion(s32[8192]{0:T(1024)S(1)} %compare_select_fusion.2, f32[8192]{0:T(1024)S(1)} %and_select_fusion, f32[]{:T(128)} %constant.76.clone.1), kind=kCustom, calls=%fused_computation.290 | custom fusion | flops 8192 | bytes 32772 | tf_op jit(solution)/shard_map/scatter-add | solution.py:129
  470.9 109.2 %psum.30 = f32[8192]{0:T(1024)S(1)} all-reduce(f32[8192]{0:T(1024)S(1)} %scatter_custom_fusion), channel_id=1, replica_groups=mesh['depth'=16,'tile'=32] {'depth','tile'}, use_global_device_ids=true, to_apply=%region_4.5 | all-reduce | flops 8192 | bytes 65536 | tf_op jit(solution)/shard_map/psum | solution.py:132
  580.1 1.7 gather_fusion.3
  582.6 1.0 gather_fusion.4
  583.6 1.0 gather_fusion.2
  584.6 1.0 fusion.12
  585.6 2.5 scatter_custom_fusion.1
  588.1 2.5 scatter_custom_fusion.2
  590.7 436.9 %all-reduce.18.cloned.1.call-done = (f32[8192]{0:T(1024)}, f32[8192]{0:T(1024)}) async-done(((f32[8192]{0:T(1024)}, f32[8192]{0:T(1024)}), (f32[8192]{0:T(1024)}, f32[8192]{0:T(1024)})) %all-reduce.18.cloned.1.call-update) | async-done | bytes 65552
  1027.6 1.3 fusion.170
  (181 shorter events, 19.8 us)
Async XLA Ops:
  7.2 171.5 %all-reduce.14.cloned.1.call-start = ((), (), s32[]{:S(2)}) async-start(), calls=%async_computation | async-start | bytes 131072 | tf_op jit(solution)/shard_map/psum | solution.py:105
  8.7 16.3 %collective-permute-start = (bf16[1,6,1024]{2,1,0:T(8,128)(2,1)}, bf16[1,6,1024]{2,1,0:T(8,128)(2,1)}, u32[]{:S(2)}, u32[]{:S(2)}) collective-permute-start(bf16[1,6,1024]{2,1,0:T(8,128)(2,1)} %get-tuple-element.46), channel_id=1, source_target_pairs={{0,1},{1,2},{2,3},{3,4},{4,5},{5,6},{6,7},{7,8},{8,9},{9,10},{10,1... | collective-permute-start | bytes 36872 | tf_op jit(solution)/shard_map/ppermute | solution.py:20
  13.3 11.8 %collective-permute-start.1 = (bf16[1,6,1024]{2,1,0:T(8,128)(2,1)}, bf16[1,6,1024]{2,1,0:T(8,128)(2,1)}, u32[]{:S(2)}, u32[]{:S(2)}) collective-permute-start(bf16[1,6,1024]{2,1,0:T(8,128)(2,1)} %get-tuple-element.47), channel_id=1, source_target_pairs={{1,0},{2,1},{3,2},{4,3},{5,4},{6,5},{7,6},{8,7},{9,8},{10,9},{11,1... | collective-permute-start | bytes 36872 | tf_op jit(solution)/shard_map/ppermute | solution.py:22
  16.3 2.7 copy-start.26
  19.0 7.5 copy-start.6
  19.0 7.7 copy-start.4
  20.0 3.3 copy-start.1
  20.0 3.2 copy-start.30
  20.0 5.0 copy-start.25
  20.0 5.0 copy-start.27
  27.8 1.9 copy-start.29
  27.9 150.8 %copy-start.8 = (f32[32,1024]{1,0:T(8,128)S(1)}, f32[32,1024]{1,0:T(8,128)}, u32[]{:S(2)}) copy-start(f32[32,1024]{1,0:T(8,128)} %param.11) | copy-start | bytes 393220
  29.7 320.5 %all-reduce.16.cloned.1.call-start = ((), (), s32[]{:S(2)}) async-start(), calls=%async_computation.1 | async-start | bytes 131072 | tf_op jit(solution)/shard_map/psum | solution.py:105
  179.5 10.2 copy-start.21
  179.5 4.2 collective-permute-start.2
  181.9 5.2 collective-permute-start.3
  187.2 3.1 copy-start.19
  188.5 2.2 copy-start.17
  191.3 1.3 copy-start.2
  192.5 10.3 copy-start.7
  193.3 9.8 copy-start.5
  193.3 5.7 collective-permute-start.4
  197.7 4.5 collective-permute-start.5
  204.2 150.6 %copy-start.3 = (bf16[1,256,4,128]{3,2,1,0:T(4,128)(2,1)S(1)}, bf16[1,256,4,128]{3,2,1,0:T(4,128)(2,1)}, u32[]{:S(2)}) copy-start(bf16[1,256,4,128]{3,2,1,0:T(4,128)(2,1)} %param.15) | copy-start | bytes 786436
  205.3 153.3 %copy-start.24 = (bf16[1,1,384,128]{3,1,2,0:T(2,128)(2,1)S(1)}, bf16[1,1,384,128]{3,1,2,0:T(2,128)(2,1)}, u32[]{:S(2)}) copy-start(bf16[1,1,384,128]{3,1,2,0:T(2,128)(2,1)} %get-tuple-element.18) | copy-start | bytes 294916
  206.0 821.6 %all-reduce.18.cloned.1.call-start = ((), (), s32[]{:S(2)}) async-start(), calls=%async_computation.2 | async-start | bytes 131072
  351.0 3.9 collective-permute-start.6
  353.2 5.2 collective-permute-start.7
  354.8 4.1 copy-start.23
  354.9 4.2 copy-start.22
  362.6 219.9 %copy-start = (f32[1,32,1024]{2,1,0:T(8,128)}, f32[1,32,1024]{2,1,0:T(8,128)S(1)}, u32[]{:S(2)}) copy-start(f32[1,32,1024]{2,1,0:T(8,128)S(1)} %fusion.44) | copy-start | bytes 393220
  362.6 65.0 %copy-start.28 = (s32[8192]{0:T(1024)S(1)}, s32[8192]{0:T(1024)}, u32[]{:S(2)}) copy-start(s32[8192]{0:T(1024)} %param.16) | copy-start | bytes 98308
  (10 other events, 10.5 us)
Sparse Core Ops, SparseCore 0:
  29.8 148.7 all-reduce.13
  206.1 144.0 all-reduce.15
  590.8 436.7 all-reduce.17
where the time goes:
time: 1040 us
  waiting for transfers between devices  740 us (71%)
  blocking collectives  109 us (10%)
  local copies, waits for them, and re-layouts  79.5 us (8%)
  other arithmetic  56.6 us (5%)
  starting transfers between devices  18.9 us (2%)
  matrix products  16.2 us (2%)
  between operations  15.1 us (1%)
    unnamed x4, waiting for transfers between devices  437 us
    psum x2, waiting for transfers between devices, body(): lax.psum(partial_value.astype(jnp.bfloat16), 'depth').astype(jnp.float32)  293 us
    psum x1, blocking collectives, body(): proj_all, seed_all = lax.psum((proj_dense, seed_dense), ('depth', 'tile'))  109 us
    gather x1, local copies, waits for them, and re-layouts, body(): estimate[seed_plane % planes_dev, seed_row % rows_dev, seed_col]  65 us
    scatter-add x1, other arithmetic, body(): jnp.zeros((neurons,), jnp.float32).at[owner_slot].add(seed_value)  43.2 us
  transfers between devices with their start and end apart: 11, of which 6 were waited for; matrix products, arithmetic and copies ran while one was open for 1% of the time, Pallas kernels for 0%

commit v1 on v0

--- a/solution.py
+++ b/solution.py
@@ -129,7 +129,7 @@
     seed_dense = jnp.zeros((neurons,), jnp.float32).at[owner_slot].add(seed_value)
     group = lax.axis_size(("depth", "tile"))
     owned_count = neurons // group
-    proj_all, seed_all = lax.psum((proj_dense, seed_dense), ("depth", "tile"))
+    proj_all, seed_all = lax.psum(lax.psum((proj_dense, seed_dense), "tile"), "depth")
     offset = lax.axis_index(("depth", "tile")) * owned_count
     proj_own = lax.dynamic_slice_in_dim(proj_all, offset, owned_count, 0)
     seed_own = lax.dynamic_slice_in_dim(seed_all, offset, owned_count, 0)

time: 1040 us -> 961 us (0.924)
  waiting for transfers between devices: 740 us -> 304 us
  blocking collectives: 109 us -> 475 us
    unnamed x4 -> x2, waiting for transfers between devices: 437 us -> 0.03 us
    psum x1 -> x4, blocking collectives: 109 us -> 368 us  [the longest x2 185 us: body(): lax.psum((proj_dense, seed_dense), 'tile')]
    unnamed x0 -> x1, blocking collectives: none -> 107 us
  transfers between devices with their start and end apart: 11 -> 10, of which waited for: 6 -> 5; matrix products, arithmetic and copies ran while one was open for 1% -> 1% of each run, Pallas kernels for 0% -> 0%
where the time goes in v1:
time: 961 us; the launch traced here: 960 us
  blocking collectives  475 us (49%)
  waiting for transfers between devices  304 us (32%)
  local copies, waits for them, and re-layouts  79.5 us (8%)
  other arithmetic  54.8 us (6%)
  starting transfers between devices  18.3 us (2%)
  between operations  15.5 us (2%)
  matrix products  14.3 us (1%)
    psum x2, waiting for transfers between devices, body(): lax.psum(partial_value.astype(jnp.bfloat16), 'depth').astype(jnp.float32)  294 us
    psum x2, blocking collectives, body(): lax.psum((proj_dense, seed_dense), 'tile')  185 us
    psum x2, blocking collectives, body(): lax.psum(lax.psum((proj_dense, seed_dense), 'tile'), 'depth')  183 us
    unnamed x1, blocking collectives  107 us
    gather x1, local copies, waits for them, and re-layouts, body(): estimate[seed_plane % planes_dev, seed_row % rows_dev, seed_col]  65 us
    scatter-add x1, other arithmetic, body(): jnp.zeros((neurons,), jnp.float32).at[owner_slot].add(seed_value)  43.4 us
  transfers between devices with their start and end apart: 10, of which 5 were waited for; matrix products, arithmetic and copies ran while one was open for 1% of the time, Pallas kernels for 0%

profile of v1, /device:TPU:1, one launch (start us, length us, event | category | flops | bytes accessed | tf_op | source)
XLA Modules:
  0.0 960.4 jit_solution(744111864881720757)
XLA Ops:
  7.2 0.9 convert_element_type.84
  8.7 3.9 collective-permute-start
  12.7 1.3 collective-permute-start.1
  14.1 1.6 fusion.7
  15.7 2.7 fusion.173
  18.5 0.9 fusion.6
  19.4 3.2 fusion.172
  23.3 1.7 gather_fusion.1
  29.0 149.5 %all-reduce.12.cloned.1.call-done = bf16[32,1024]{1,0:T(8,128)(2,1)} async-done(((bf16[32,1024]{1,0:T(8,128)(2,1)}), bf16[32,1024]{1,0:T(8,128)(2,1)}) %all-reduce.12.cloned.1.call-update) | async-done | bytes 65552 | tf_op jit(solution)/shard_map/psum | solution.py:105
  179.4 2.3 collective-permute-start.2
  181.7 1.3 collective-permute-start.3
  183.6 3.3 collective-permute-done.3
  191.2 4.4 collective-permute-start.4
  195.6 1.3 collective-permute-start.5
  197.0 3.1 collective-permute-done.5
  204.0 144.2 %all-reduce.14.cloned.1.call-done = bf16[32,1024]{1,0:T(8,128)(2,1)} async-done(((bf16[32,1024]{1,0:T(8,128)(2,1)}), bf16[32,1024]{1,0:T(8,128)(2,1)}) %all-reduce.14.cloned.1.call-update) | async-done | bytes 65552 | tf_op jit(solution)/shard_map/psum | solution.py:105
  349.0 2.2 collective-permute-start.6
  351.2 1.5 collective-permute-start.7
  352.9 3.5 collective-permute-done.7
  360.5 65.0 %gather_fusion = f32[8192]{0:T(1024)S(1)} fusion(f32[1,32,1024]{2,1,0:T(8,128)S(1)} %fusion.44, s32[8192]{0:T(1024)S(1)} %fusion.156), kind=kCustom, calls=%fused_computation | custom fusion | bytes 163840 | tf_op jit(solution)/shard_map/gather | solution.py:126
  425.6 43.4 %scatter_custom_fusion = f32[8192]{0:T(1024)S(1)} fusion(s32[8192]{0:T(1024)} %compare_select_fusion.2, f32[8192]{0:T(1024)S(1)} %and_select_fusion, f32[]{:T(128)} %constant.76.clone.1), kind=kCustom, calls=%fused_computation.290 | custom fusion | flops 8192 | bytes 33280 | tf_op jit(solution)/shard_map/scatter-add | solution.py:129
  469.0 94.4 %psum.44 = f32[8192]{0:T(1024)S(1)} all-reduce(f32[8192]{0:T(1024)S(1)} %scatter_custom_fusion), channel_id=1, replica_groups=mesh['depth'=16,'tile'=32] {'tile'}, use_global_device_ids=true, to_apply=%region_4.5 | all-reduce | flops 8192 | bytes 65536 | tf_op jit(solution)/shard_map/psum | solution.py:132
  563.4 90.3 %psum.45 = f32[8192]{0:T(1024)S(1)} all-reduce(f32[8192]{0:T(1024)S(1)} %psum.44), channel_id=1, replica_groups=mesh['depth'=16,'tile'=32] {'depth'}, use_global_device_ids=true, to_apply=%region_5.6 | all-reduce | flops 8192 | bytes 65536 | tf_op jit(solution)/shard_map/psum | solution.py:132
  653.7 1.7 gather_fusion.3
  656.2 1.0 gather_fusion.4
  657.2 1.0 gather_fusion.2
  658.2 1.0 fusion.12
  659.2 2.0 scatter_custom_fusion.1
  661.2 90.8 %psum.46 = f32[8192]{0:T(1024)S(1)} all-reduce(f32[8192]{0:T(1024)S(1)} %scatter_custom_fusion.1), channel_id=1, replica_groups=mesh['depth'=16,'tile'=32] {'tile'}, use_global_device_ids=true, to_apply=%region_8.9 | all-reduce | flops 8192 | bytes 65536 | tf_op jit(solution)/shard_map/psum | solution.py:132
  752.1 92.4 %psum.47 = f32[8192]{0:T(1024)S(1)} all-reduce(f32[8192]{0:T(1024)S(1)} %psum.46), channel_id=1, replica_groups=mesh['depth'=16,'tile'=32] {'depth'}, use_global_device_ids=true, to_apply=%region_9.10 | all-reduce | flops 8192 | bytes 65536 | tf_op jit(solution)/shard_map/psum | solution.py:132
  844.5 2.0 scatter_custom_fusion.2
  846.5 106.5 %all-reduce.8 = f32[8192]{0:T(1024)S(1)} all-reduce(f32[8192]{0:T(1024)S(1)} %scatter_custom_fusion.2), channel_id=2, replica_groups=mesh['depth'=16,'tile'=32] {'depth','tile'}, use_global_device_ids=true, to_apply=%region_12.13.clone | all-reduce | flops 8192 | bytes 65536
  (188 shorter events, 20.6 us)
Async XLA Ops:
  7.2 171.3 %all-reduce.12.cloned.1.call-start = ((), (), s32[]{:S(2)}) async-start(), calls=%async_computation | async-start | bytes 131072 | tf_op jit(solution)/shard_map/psum | solution.py:105
  8.7 16.3 %collective-permute-start = (bf16[1,6,1024]{2,1,0:T(8,128)(2,1)}, bf16[1,6,1024]{2,1,0:T(8,128)(2,1)S(1)}, u32[]{:S(2)}, u32[]{:S(2)}) collective-permute-start(bf16[1,6,1024]{2,1,0:T(8,128)(2,1)} %get-tuple-element.44), channel_id=1, source_target_pairs={{0,1},{1,2},{2,3},{3,4},{4,5},{5,6},{6,7},{7,8},{8,9},{9,10},{10,1... | collective-permute-start | bytes 36872 | tf_op jit(solution)/shard_map/ppermute | solution.py:20
  12.7 12.4 %collective-permute-start.1 = (bf16[1,6,1024]{2,1,0:T(8,128)(2,1)}, bf16[1,6,1024]{2,1,0:T(8,128)(2,1)S(1)}, u32[]{:S(2)}, u32[]{:S(2)}) collective-permute-start(bf16[1,6,1024]{2,1,0:T(8,128)(2,1)} %get-tuple-element.45), channel_id=1, source_target_pairs={{1,0},{2,1},{3,2},{4,3},{5,4},{6,5},{7,6},{8,7},{9,8},{10,9},{11,1... | collective-permute-start | bytes 36872 | tf_op jit(solution)/shard_map/ppermute | solution.py:22
  15.7 2.7 copy-start.28
  18.4 7.3 copy-start.6
  18.4 7.5 copy-start.4
  19.4 3.2 copy-start.1
  19.4 3.8 copy-start.32
  19.4 5.6 copy-start.27
  19.4 5.6 copy-start.29
  27.1 1.9 copy-start.31
  27.1 151.4 %copy-start.8 = (f32[32,1024]{1,0:T(8,128)S(1)}, f32[32,1024]{1,0:T(8,128)}, u32[]{:S(2)}) copy-start(f32[32,1024]{1,0:T(8,128)} %param.11) | copy-start | bytes 393220
  27.8 159.3 %copy-start.25 = (bf16[1,1,384,128]{3,1,2,0:T(2,128)(2,1)S(1)}, bf16[1,1,384,128]{3,1,2,0:T(2,128)(2,1)}, u32[]{:S(2)}) copy-start(bf16[1,1,384,128]{3,1,2,0:T(2,128)(2,1)} %get-tuple-element.16) | copy-start | bytes 294916
  28.3 159.1 %copy-start.23 = (bf16[1,1,384,128]{3,1,2,0:T(2,128)(2,1)S(1)}, bf16[1,1,384,128]{3,1,2,0:T(2,128)(2,1)}, u32[]{:S(2)}) copy-start(bf16[1,1,384,128]{3,1,2,0:T(2,128)(2,1)} %get-tuple-element.15) | copy-start | bytes 294916
  28.9 319.2 %all-reduce.14.cloned.1.call-start = ((), (), s32[]{:S(2)}) async-start(), calls=%async_computation.1 | async-start | bytes 131072 | tf_op jit(solution)/shard_map/psum | solution.py:105
  179.4 8.2 copy-start.21
  179.4 4.2 collective-permute-start.2
  181.7 5.2 collective-permute-start.3
  189.3 1.3 copy-start.2
  189.5 7.5 copy-start.33
  190.4 10.3 %copy-start.7 = (bf16[1,1,384,128]{3,1,2,0:T(2,128)(2,1)S(1)}, bf16[1,1,384,128]{3,1,2,0:T(2,128)(2,1)}, u32[]{:S(2)}) copy-start(bf16[1,1,384,128]{3,1,2,0:T(2,128)(2,1)} %copy-done.6) | copy-start | bytes 294916
  191.2 9.8 %copy-start.5 = (bf16[1,1,384,128]{3,1,2,0:T(2,128)(2,1)S(1)}, bf16[1,1,384,128]{3,1,2,0:T(2,128)(2,1)}, u32[]{:S(2)}) copy-start(bf16[1,1,384,128]{3,1,2,0:T(2,128)(2,1)} %copy-done.4) | copy-start | bytes 294916
  191.2 5.7 collective-permute-start.4
  195.6 4.5 collective-permute-start.5
  202.1 150.6 %copy-start.3 = (bf16[1,256,4,128]{3,2,1,0:T(4,128)(2,1)S(1)}, bf16[1,256,4,128]{3,2,1,0:T(4,128)(2,1)}, u32[]{:S(2)}) copy-start(bf16[1,256,4,128]{3,2,1,0:T(4,128)(2,1)} %param.15) | copy-start | bytes 786436
  203.3 153.3 %copy-start.26 = (bf16[1,1,384,128]{3,1,2,0:T(2,128)(2,1)S(1)}, bf16[1,1,384,128]{3,1,2,0:T(2,128)(2,1)}, u32[]{:S(2)}) copy-start(bf16[1,1,384,128]{3,1,2,0:T(2,128)(2,1)} %get-tuple-element.16) | copy-start | bytes 294916
  349.0 3.9 collective-permute-start.6
  351.2 5.2 collective-permute-start.7
  352.7 4.1 copy-start.24
  352.9 4.2 copy-start.22
  360.5 295.5 %copy-start = (f32[1,32,1024]{2,1,0:T(8,128)}, f32[1,32,1024]{2,1,0:T(8,128)S(1)}, u32[]{:S(2)}) copy-start(f32[1,32,1024]{2,1,0:T(8,128)S(1)} %fusion.44) | copy-start | bytes 393220
  360.5 65.0 %copy-start.30 = (s32[8192]{0:T(1024)S(1)}, s32[8192]{0:T(1024)}, u32[]{:S(2)}) copy-start(s32[8192]{0:T(1024)} %param.16) | copy-start | bytes 98308
  (12 other events, 13.0 us)
Sparse Core Ops, SparseCore 0:
  29.1 149.3 all-reduce.11
  204.1 144.0 all-reduce.13
